TPU v7x, 32 devices: a whole 2x2x4 slice. The times are simulated.
32 devices in a mesh: parts: 2 (over y), span: 4 (over x, core), seq: 4 (over z).
Axes of the slice: x: 2, y: 2, z: 4, core: 2. Of those that a mesh axis runs over, the one named last changes fastest.
Arguments:
- q_in: bfloat16 [8, 1024, 4096], P(('parts', 'span'), 'seq'), parts along dimension 0, may hold values from -9 to 9
- k_in: bfloat16 [8, 1024, 4096], P(('parts', 'span'), 'seq'), parts along dimension 0, may hold values from -9 to 9
- v_in: bfloat16 [8, 1024, 4096], P(('parts', 'span'), 'seq'), parts along dimension 0, may hold values from -18 to 18
- timesteps: int32 [8], P('parts'), parts along dimension 0, may hold values from 0 to 31
- gate_table: float32 [32, 4096], replicated, may hold values from 0.1 to 1.9
Outputs:
- gated_out: bfloat16 [8, 1024, 4096], P(('parts', 'span'), 'seq'), parts along dimension 0
There are 2 independent parts, one for each index of `parts`. A program takes and returns all parts, laid end to end along the dimension named above; an argument that names none is the same for every part. Nothing has to cross between parts.
All inputs are finite; a program needn't handle non-finite values.
Results may differ from a plain program's by a relative error of at most 0.0053.
Values may be sent and summed in bfloat16 or wider, within the bound.
A program may use at most 128 MiB of HBM per device.

v0:
```python
import math
import jax
import jax.numpy as jnp
from jax import lax
from jax.sharding import PartitionSpec as P

HD = 128
masked_score = -1e30


def local(q_in, k_in, v_in, timesteps, gate_table):
    head_rows, key_rows, value_rows = (
        lax.all_to_all(q_in[0], "seq", split_axis=1, concat_axis=0, tiled=True),
        lax.all_to_all(k_in[0], "seq", split_axis=1, concat_axis=0, tiled=True),
        lax.all_to_all(v_in[0], "seq", split_axis=1, concat_axis=0, tiled=True),
    )
    length = head_rows.shape[0]
    columns = head_rows.shape[1]
    heads = columns // HD
    scale = HD ** (-0.5)
    span_id = lax.axis_index("span")
    limit = (span_id + 1) * length
    query_three = head_rows.reshape(length, heads, HD)
    init = (
        jnp.full((heads, length), masked_score, jnp.float32),
        jnp.zeros((heads, length), jnp.float32),
        jnp.zeros((length, heads, HD), jnp.float32),
    )
    key_piece = lax.all_gather(key_rows, "span", axis=0, tiled=True)
    value_piece = lax.all_gather(value_rows, "span", axis=0, tiled=True)
    count = key_piece.shape[0]
    block = math.gcd(count, 512)

    def one_block(index, state):
        top, total, accum = state
        offset = index * block
        key_block = lax.dynamic_slice_in_dim(key_piece, offset, block, 0).reshape(block, heads, HD)
        value_block = lax.dynamic_slice_in_dim(value_piece, offset, block, 0).reshape(
            block, heads, HD
        )
        scores = (
            jnp.einsum("qhd,khd->hqk", query_three, key_block, preferred_element_type=jnp.float32)
            * scale
        )
        keep = offset + jnp.arange(block) < limit
        scores = jnp.where(keep[None, None, :], scores, masked_score)
        new_top = jnp.maximum(top, jnp.max(scores, axis=-1))
        expo = jnp.where(keep[None, None, :], jnp.exp(scores - new_top[:, :, None]), 0.0)
        shrink = jnp.exp(top - new_top)
        total = total * shrink + jnp.sum(expo, axis=-1)
        mixed = jnp.einsum(
            "hqk,khd->qhd",
            expo.astype(jnp.bfloat16),
            value_block,
            preferred_element_type=jnp.float32,
        )
        accum = accum * shrink.T[:, :, None] + mixed
        return (new_top, total, accum)

    def run_blocks(state):
        return lax.fori_loop(0, count // block, one_block, state)

    def keep_state(state):
        return state

    top, total, accum = lax.cond(jnp.int32(0) < limit, run_blocks, keep_state, init)
    attn = (accum / total.T[:, :, None]).reshape(length, columns).astype(jnp.bfloat16)
    token_rows = lax.all_to_all(attn, "seq", split_axis=0, concat_axis=1, tiled=True)
    steps_count = gate_table.shape[0]
    span_step = lax.dynamic_index_in_dim(timesteps, span_id, 0, keepdims=False)
    picked = (jnp.arange(steps_count) == span_step).astype(jnp.float32)
    gate = jnp.dot(picked, gate_table, precision=lax.Precision.HIGHEST)
    return (token_rows.astype(jnp.float32) * gate[None, :]).astype(jnp.bfloat16)[None]


def solution(mesh):
    in_specs = (
        P(("parts", "span"), "seq", None),
        P(("parts", "span"), "seq", None),
        P(("parts", "span"), "seq", None),
        P("parts"),
        P(),
    )
    out_specs = P(("parts", "span"), "seq", None)
    return jax.shard_map(local, mesh=mesh, in_specs=in_specs, out_specs=out_specs, check_vma=False)
```

profile of v0, /device:TPU:0, one launch (start us, length us, event | category | flops | bytes accessed | tf_op | source)
XLA Modules:
  0.0 533.7 jit_solution(13859830746761117424)
XLA Ops:
  10.7 54.5 %all_to_all.64 = bf16[256,4,1024]{0,2,1:T(8,128)(2,1)S(1)} all-to-all(bf16[256,4,1024]{0,2,1:T(8,128)(2,1)} %bitcast.80), channel_id=1, replica_groups=mesh['parts'=2,'span'=4,'seq'=4] {'seq'}, dimensions={1} | all-to-all | bytes 4194304 | tf_op jit(solution)/shard_map/all_to_all | solution.py:14
  71.8 51.0 %all_to_all.65 = bf16[256,4,1024]{0,2,1:T(8,128)(2,1)S(1)} all-to-all(bf16[256,4,1024]{0,2,1:T(8,128)(2,1)} %bitcast.81), channel_id=1, replica_groups=mesh['parts'=2,'span'=4,'seq'=4] {'seq'}, dimensions={1} | all-to-all | bytes 4194304 | tf_op jit(solution)/shard_map/all_to_all | solution.py:15
  132.9 47.3 %all-to-all-done = bf16[256,4,1024]{0,2,1:T(8,128)(2,1)S(1)} async-done(((bf16[256,4,1024]{0,2,1:T(8,128)(2,1)}), bf16[256,4,1024]{0,2,1:T(8,128)(2,1)S(1)}, u32[]{:S(2)}, u32[]{:S(2)}) %all-to-all-start) | async-done | bytes 2097184 | tf_op jit(solution)/shard_map/all_to_all | solution.py:13
  180.2 5.0 all-gather.5.cloned.1.call-done
  185.2 271.6 %conditional.1 = (f32[8,1024]{1,0:T(8,128)}, f32[1024,8,128]{0,2,1:T(8,128)}) conditional(s32[]{:T(128)} %convert_element_type.44, () %tuple.27, (bf16[4,256,1024]{1,2,0:T(8,128)(2,1)S(1)}, s32[]{:T(128)}, bf16[4096,1024]{1,0:T(8,128)(2,1)}, bf16[4096,1024]{1,0:T(8,128)(2,1)}) %tuple.65), branch_computations={%region_0.0_spmd, %region_1.6_spmd} | conditional | flops 2205205504 | bytes 151521616 | solution.py:66
  191.5 265.3 %while.17 = (s32[]{:T(128)}, f32[8,1024]{1,0:T(8,128)S(1)}, f32[8,1024]{1,0:T(8,128)}, f32[1024,8,128]{0,2,1:T(8,128)}, s32[]{:T(128)}, /*index=5*/bf16[4096,102...) while((s32[]{:T(128)}, f32[8,1024]{1,0:T(8,128)S(1)}, ...), condition=%wide.region_5.5_spmd.clone, body=%wide.region_2.4_spmd.clone.sunk | while | flops 2205205504 | bytes 138938576 | solution.py:61
  195.7 9.4 %bitcast_reduce_fusion.2 = (f32[8,1024]{1,0:T(8,128)S(1)}, f32[8,512,1024]{2,1,0:T(8,128)}) fusion(pred[512]{0:T(512)(128)(4,1)S(1)} %add_compare_fusion.2, bf16[512,8,128]{0,2,1:T(8,128)(2,1)S(1)} %bitcast.72, bf16[1024,8,128]{2,0,1:T(8,128)(2,1)} %get-tuple-element.338), kind=kOutput, calls=%fused_computation.1.clone.1 | convolution fusion | flops 1086316544 | bytes 19956224 | tf_op jit(solution)/shard_map/cond/branch_1_fun/while/body/eval_jaxpr/qhd,khd->hqk/dot_general | solution.py:42
  205.6 10.9 %bitcast_add_fusion.2 = f32[1024,8,128]{0,2,1:T(8,128)} fusion(f32[1024,8,128]{0,2,1:T(8,128)} %get-tuple-element.323, bf16[512,8,128]{0,2,1:T(8,128)(2,1)S(1)} %bitcast.73, f32[8,512,1024]{2,1,0:T(8,128)} %get-tuple-element.305, f32[8,1024]{1,0:T(8,128)S(1)} %get-tuple-element.333, pred[512]{0:T(512)(128)(4,1)S(1)} %add_compare_fusion.2, ...), kind=kOutput, calls=%fused_computation.10.clone.1 | convolution fusion | flops 1097859072 | bytes 26280448 | tf_op jit(solution)/shard_map/cond/branch_1_fun/while/body/eval_jaxpr/hqk,khd->qhd/dot_general | solution.py:51
  217.7 4.6 fusion.37
  227.1 9.4 %bitcast_reduce_fusion.2 = (f32[8,1024]{1,0:T(8,128)S(1)}, f32[8,512,1024]{2,1,0:T(8,128)}) fusion(pred[512]{0:T(512)(128)(4,1)S(1)} %add_compare_fusion.2, bf16[512,8,128]{0,2,1:T(8,128)(2,1)S(1)} %bitcast.72, bf16[1024,8,128]{2,0,1:T(8,128)(2,1)} %get-tuple-element.338), kind=kOutput, calls=%fused_computation.1.clone.1 | convolution fusion | flops 1086316544 | bytes 19956224 | tf_op jit(solution)/shard_map/cond/branch_1_fun/while/body/eval_jaxpr/qhd,khd->hqk/dot_general | solution.py:42
  237.1 12.1 %bitcast_add_fusion.2 = f32[1024,8,128]{0,2,1:T(8,128)} fusion(f32[1024,8,128]{0,2,1:T(8,128)} %get-tuple-element.323, bf16[512,8,128]{0,2,1:T(8,128)(2,1)S(1)} %bitcast.73, f32[8,512,1024]{2,1,0:T(8,128)} %get-tuple-element.305, f32[8,1024]{1,0:T(8,128)S(1)} %get-tuple-element.333, pred[512]{0:T(512)(128)(4,1)S(1)} %add_compare_fusion.2, ...), kind=kOutput, calls=%fused_computation.10.clone.1 | convolution fusion | flops 1097859072 | bytes 26280448 | tf_op jit(solution)/shard_map/cond/branch_1_fun/while/body/eval_jaxpr/hqk,khd->qhd/dot_general | solution.py:51
  250.3 4.6 fusion.37
  260.5 9.4 %bitcast_reduce_fusion.2 = (f32[8,1024]{1,0:T(8,128)S(1)}, f32[8,512,1024]{2,1,0:T(8,128)}) fusion(pred[512]{0:T(512)(128)(4,1)S(1)} %add_compare_fusion.2, bf16[512,8,128]{0,2,1:T(8,128)(2,1)S(1)} %bitcast.72, bf16[1024,8,128]{2,0,1:T(8,128)(2,1)} %get-tuple-element.338), kind=kOutput, calls=%fused_computation.1.clone.1 | convolution fusion | flops 1086316544 | bytes 19956224 | tf_op jit(solution)/shard_map/cond/branch_1_fun/while/body/eval_jaxpr/qhd,khd->hqk/dot_general | solution.py:42
  270.5 12.1 %bitcast_add_fusion.2 = f32[1024,8,128]{0,2,1:T(8,128)} fusion(f32[1024,8,128]{0,2,1:T(8,128)} %get-tuple-element.323, bf16[512,8,128]{0,2,1:T(8,128)(2,1)S(1)} %bitcast.73, f32[8,512,1024]{2,1,0:T(8,128)} %get-tuple-element.305, f32[8,1024]{1,0:T(8,128)S(1)} %get-tuple-element.333, pred[512]{0:T(512)(128)(4,1)S(1)} %add_compare_fusion.2, ...), kind=kOutput, calls=%fused_computation.10.clone.1 | convolution fusion | flops 1097859072 | bytes 26280448 | tf_op jit(solution)/shard_map/cond/branch_1_fun/while/body/eval_jaxpr/hqk,khd->qhd/dot_general | solution.py:51
  283.7 4.6 fusion.37
  293.9 9.4 %bitcast_reduce_fusion.2 = (f32[8,1024]{1,0:T(8,128)S(1)}, f32[8,512,1024]{2,1,0:T(8,128)}) fusion(pred[512]{0:T(512)(128)(4,1)S(1)} %add_compare_fusion.2, bf16[512,8,128]{0,2,1:T(8,128)(2,1)S(1)} %bitcast.72, bf16[1024,8,128]{2,0,1:T(8,128)(2,1)} %get-tuple-element.338), kind=kOutput, calls=%fused_computation.1.clone.1 | convolution fusion | flops 1086316544 | bytes 19956224 | tf_op jit(solution)/shard_map/cond/branch_1_fun/while/body/eval_jaxpr/qhd,khd->hqk/dot_general | solution.py:42
  303.9 12.1 %bitcast_add_fusion.2 = f32[1024,8,128]{0,2,1:T(8,128)} fusion(f32[1024,8,128]{0,2,1:T(8,128)} %get-tuple-element.323, bf16[512,8,128]{0,2,1:T(8,128)(2,1)S(1)} %bitcast.73, f32[8,512,1024]{2,1,0:T(8,128)} %get-tuple-element.305, f32[8,1024]{1,0:T(8,128)S(1)} %get-tuple-element.333, pred[512]{0:T(512)(128)(4,1)S(1)} %add_compare_fusion.2, ...), kind=kOutput, calls=%fused_computation.10.clone.1 | convolution fusion | flops 1097859072 | bytes 26280448 | tf_op jit(solution)/shard_map/cond/branch_1_fun/while/body/eval_jaxpr/hqk,khd->qhd/dot_general | solution.py:51
  317.1 4.6 fusion.37
  327.4 9.4 %bitcast_reduce_fusion.2 = (f32[8,1024]{1,0:T(8,128)S(1)}, f32[8,512,1024]{2,1,0:T(8,128)}) fusion(pred[512]{0:T(512)(128)(4,1)S(1)} %add_compare_fusion.2, bf16[512,8,128]{0,2,1:T(8,128)(2,1)S(1)} %bitcast.72, bf16[1024,8,128]{2,0,1:T(8,128)(2,1)} %get-tuple-element.338), kind=kOutput, calls=%fused_computation.1.clone.1 | convolution fusion | flops 1086316544 | bytes 19956224 | tf_op jit(solution)/shard_map/cond/branch_1_fun/while/body/eval_jaxpr/qhd,khd->hqk/dot_general | solution.py:42
  337.3 12.1 %bitcast_add_fusion.2 = f32[1024,8,128]{0,2,1:T(8,128)} fusion(f32[1024,8,128]{0,2,1:T(8,128)} %get-tuple-element.323, bf16[512,8,128]{0,2,1:T(8,128)(2,1)S(1)} %bitcast.73, f32[8,512,1024]{2,1,0:T(8,128)} %get-tuple-element.305, f32[8,1024]{1,0:T(8,128)S(1)} %get-tuple-element.333, pred[512]{0:T(512)(128)(4,1)S(1)} %add_compare_fusion.2, ...), kind=kOutput, calls=%fused_computation.10.clone.1 | convolution fusion | flops 1097859072 | bytes 26280448 | tf_op jit(solution)/shard_map/cond/branch_1_fun/while/body/eval_jaxpr/hqk,khd->qhd/dot_general | solution.py:51
  350.5 4.6 fusion.37
  360.8 9.4 %bitcast_reduce_fusion.2 = (f32[8,1024]{1,0:T(8,128)S(1)}, f32[8,512,1024]{2,1,0:T(8,128)}) fusion(pred[512]{0:T(512)(128)(4,1)S(1)} %add_compare_fusion.2, bf16[512,8,128]{0,2,1:T(8,128)(2,1)S(1)} %bitcast.72, bf16[1024,8,128]{2,0,1:T(8,128)(2,1)} %get-tuple-element.338), kind=kOutput, calls=%fused_computation.1.clone.1 | convolution fusion | flops 1086316544 | bytes 19956224 | tf_op jit(solution)/shard_map/cond/branch_1_fun/while/body/eval_jaxpr/qhd,khd->hqk/dot_general | solution.py:42
  370.7 12.1 %bitcast_add_fusion.2 = f32[1024,8,128]{0,2,1:T(8,128)} fusion(f32[1024,8,128]{0,2,1:T(8,128)} %get-tuple-element.323, bf16[512,8,128]{0,2,1:T(8,128)(2,1)S(1)} %bitcast.73, f32[8,512,1024]{2,1,0:T(8,128)} %get-tuple-element.305, f32[8,1024]{1,0:T(8,128)S(1)} %get-tuple-element.333, pred[512]{0:T(512)(128)(4,1)S(1)} %add_compare_fusion.2, ...), kind=kOutput, calls=%fused_computation.10.clone.1 | convolution fusion | flops 1097859072 | bytes 26280448 | tf_op jit(solution)/shard_map/cond/branch_1_fun/while/body/eval_jaxpr/hqk,khd->qhd/dot_general | solution.py:51
  383.9 4.6 fusion.37
  394.2 9.4 %bitcast_reduce_fusion.2 = (f32[8,1024]{1,0:T(8,128)S(1)}, f32[8,512,1024]{2,1,0:T(8,128)}) fusion(pred[512]{0:T(512)(128)(4,1)S(1)} %add_compare_fusion.2, bf16[512,8,128]{0,2,1:T(8,128)(2,1)S(1)} %bitcast.72, bf16[1024,8,128]{2,0,1:T(8,128)(2,1)} %get-tuple-element.338), kind=kOutput, calls=%fused_computation.1.clone.1 | convolution fusion | flops 1086316544 | bytes 19956224 | tf_op jit(solution)/shard_map/cond/branch_1_fun/while/body/eval_jaxpr/qhd,khd->hqk/dot_general | solution.py:42
  404.1 12.1 %bitcast_add_fusion.2 = f32[1024,8,128]{0,2,1:T(8,128)} fusion(f32[1024,8,128]{0,2,1:T(8,128)} %get-tuple-element.323, bf16[512,8,128]{0,2,1:T(8,128)(2,1)S(1)} %bitcast.73, f32[8,512,1024]{2,1,0:T(8,128)} %get-tuple-element.305, f32[8,1024]{1,0:T(8,128)S(1)} %get-tuple-element.333, pred[512]{0:T(512)(128)(4,1)S(1)} %add_compare_fusion.2, ...), kind=kOutput, calls=%fused_computation.10.clone.1 | convolution fusion | flops 1097859072 | bytes 26280448 | tf_op jit(solution)/shard_map/cond/branch_1_fun/while/body/eval_jaxpr/hqk,khd->qhd/dot_general | solution.py:51
  417.4 4.6 fusion.37
  427.6 9.4 %bitcast_reduce_fusion.2 = (f32[8,1024]{1,0:T(8,128)S(1)}, f32[8,512,1024]{2,1,0:T(8,128)}) fusion(pred[512]{0:T(512)(128)(4,1)S(1)} %add_compare_fusion.2, bf16[512,8,128]{0,2,1:T(8,128)(2,1)S(1)} %bitcast.72, bf16[1024,8,128]{2,0,1:T(8,128)(2,1)} %get-tuple-element.338), kind=kOutput, calls=%fused_computation.1.clone.1 | convolution fusion | flops 1086316544 | bytes 19956224 | tf_op jit(solution)/shard_map/cond/branch_1_fun/while/body/eval_jaxpr/qhd,khd->hqk/dot_general | solution.py:42
  437.5 12.1 %bitcast_add_fusion.2 = f32[1024,8,128]{0,2,1:T(8,128)} fusion(f32[1024,8,128]{0,2,1:T(8,128)} %get-tuple-element.323, bf16[512,8,128]{0,2,1:T(8,128)(2,1)S(1)} %bitcast.73, f32[8,512,1024]{2,1,0:T(8,128)} %get-tuple-element.305, f32[8,1024]{1,0:T(8,128)S(1)} %get-tuple-element.333, pred[512]{0:T(512)(128)(4,1)S(1)} %add_compare_fusion.2, ...), kind=kOutput, calls=%fused_computation.10.clone.1 | convolution fusion | flops 1097859072 | bytes 26280448 | tf_op jit(solution)/shard_map/cond/branch_1_fun/while/body/eval_jaxpr/hqk,khd->qhd/dot_general | solution.py:51
  450.8 4.6 fusion.37
  466.7 4.6 all-to-all-start.3
  472.8 47.3 %all-to-all-done.3 = bf16[4,256,1024]{2,1,0:T(8,128)(2,1)} async-done(((bf16[4,256,1024]{2,1,0:T(8,128)(2,1)}), bf16[4,256,1024]{2,1,0:T(8,128)(2,1)}, u32[]{:S(2)}, u32[]{:S(2)}) %all-to-all-start.3) | async-done | bytes 2097184 | tf_op jit(solution)/shard_map/all_to_all | solution.py:68
  (102 shorter events, 103.1 us)
Async XLA Ops:
  6.5 465.3 %copy-start = (f32[32,4096]{1,0:T(8,128)S(1)}, f32[32,4096]{1,0:T(8,128)}, u32[]{:S(2)}) copy-start(f32[32,4096]{1,0:T(8,128)} %param.13) | copy-start | bytes 1572868
  6.5 173.7 %all-gather.3.cloned.1.call-start = ((), (), s32[]{:S(2)}) async-start(), calls=%async_computation.4 | async-start | bytes 10485760 | tf_op jit(solution)/shard_map/all_gather | solution.py:29
  67.7 117.5 %all-gather.5.cloned.1.call-start = ((), (), s32[]{:S(2)}) async-start(), calls=%async_computation.5 | async-start | bytes 10485760 | tf_op jit(solution)/shard_map/all_gather | solution.py:30
  129.3 50.9 %all-to-all-start = ((bf16[256,4,1024]{0,2,1:T(8,128)(2,1)}), bf16[256,4,1024]{0,2,1:T(8,128)(2,1)S(1)}, u32[]{:S(2)}, u32[]{:S(2)}) async-start(bf16[256,4,1024]{0,2,1:T(8,128)(2,1)} %bitcast.78), calls=%async_computation | async-start | bytes 4194304 | tf_op jit(solution)/shard_map/all_to_all | solution.py:13
  205.6 12.1 %copy-start.1 = (f32[8,512,1024]{2,1,0:T(8,128)S(1)}, f32[8,512,1024]{2,1,0:T(8,128)}, u32[]{:S(2)}) copy-start(f32[8,512,1024]{2,1,0:T(8,128)} %get-tuple-element.305) | copy-start | bytes 50331652 | tf_op jit(solution)/shard_map/cond/branch_1_fun/while
  237.1 13.3 %copy-start.1 = (f32[8,512,1024]{2,1,0:T(8,128)S(1)}, f32[8,512,1024]{2,1,0:T(8,128)}, u32[]{:S(2)}) copy-start(f32[8,512,1024]{2,1,0:T(8,128)} %get-tuple-element.305) | copy-start | bytes 50331652 | tf_op jit(solution)/shard_map/cond/branch_1_fun/while
  270.5 13.3 %copy-start.1 = (f32[8,512,1024]{2,1,0:T(8,128)S(1)}, f32[8,512,1024]{2,1,0:T(8,128)}, u32[]{:S(2)}) copy-start(f32[8,512,1024]{2,1,0:T(8,128)} %get-tuple-element.305) | copy-start | bytes 50331652 | tf_op jit(solution)/shard_map/cond/branch_1_fun/while
  303.9 13.3 %copy-start.1 = (f32[8,512,1024]{2,1,0:T(8,128)S(1)}, f32[8,512,1024]{2,1,0:T(8,128)}, u32[]{:S(2)}) copy-start(f32[8,512,1024]{2,1,0:T(8,128)} %get-tuple-element.305) | copy-start | bytes 50331652 | tf_op jit(solution)/shard_map/cond/branch_1_fun/while
  337.3 13.3 %copy-start.1 = (f32[8,512,1024]{2,1,0:T(8,128)S(1)}, f32[8,512,1024]{2,1,0:T(8,128)}, u32[]{:S(2)}) copy-start(f32[8,512,1024]{2,1,0:T(8,128)} %get-tuple-element.305) | copy-start | bytes 50331652 | tf_op jit(solution)/shard_map/cond/branch_1_fun/while
  370.7 13.3 %copy-start.1 = (f32[8,512,1024]{2,1,0:T(8,128)S(1)}, f32[8,512,1024]{2,1,0:T(8,128)}, u32[]{:S(2)}) copy-start(f32[8,512,1024]{2,1,0:T(8,128)} %get-tuple-element.305) | copy-start | bytes 50331652 | tf_op jit(solution)/shard_map/cond/branch_1_fun/while
  404.1 13.3 %copy-start.1 = (f32[8,512,1024]{2,1,0:T(8,128)S(1)}, f32[8,512,1024]{2,1,0:T(8,128)}, u32[]{:S(2)}) copy-start(f32[8,512,1024]{2,1,0:T(8,128)} %get-tuple-element.305) | copy-start | bytes 50331652 | tf_op jit(solution)/shard_map/cond/branch_1_fun/while
  437.5 13.3 %copy-start.1 = (f32[8,512,1024]{2,1,0:T(8,128)S(1)}, f32[8,512,1024]{2,1,0:T(8,128)}, u32[]{:S(2)}) copy-start(f32[8,512,1024]{2,1,0:T(8,128)} %get-tuple-element.305) | copy-start | bytes 50331652 | tf_op jit(solution)/shard_map/cond/branch_1_fun/while
  462.4 8.9 %copy-start.2 = (s32[4]{0:T(128)S(1)}, s32[4]{0:T(128)}, u32[]{:S(2)}) copy-start(s32[4]{0:T(128)} %param.12) | copy-start | bytes 52
  466.7 53.4 %all-to-all-start.3 = ((bf16[4,256,1024]{2,1,0:T(8,128)(2,1)}), bf16[4,256,1024]{2,1,0:T(8,128)(2,1)}, u32[]{:S(2)}, u32[]{:S(2)}) async-start(bf16[4,256,1024]{2,1,0:T(8,128)(2,1)} %copy.42), calls=%async_computation.3 | async-start | bytes 4194304 | tf_op jit(solution)/shard_map/all_to_all | solution.py:68
Sparse Core Ops, SparseCore 0:
  67.8 57.4 all-gather.2
  126.9 58.2 all-gather.4
where the time goes:
time: 536 us; the launch traced here: 534 us
  matrix products  171 us (32%)
  blocking collectives  105 us (20%)
  waiting for transfers between devices  99.6 us (19%)
  local copies, waits for them, and re-layouts  84 us (16%)
  other arithmetic  51.5 us (10%)
  between operations  13.5 us (3%)
  starting transfers between devices  8.25 us (2%)
    dot_general x8, matrix products, one_block(): jnp.einsum('hqk,khd->qhd', expo.astype(jnp.bfloat16), value_block, prefer...  95.3 us
    dot_general x8, matrix products, one_block(): jnp.einsum('qhd,khd->hqk', query_three, key_block, preferred_element_type...  74.9 us
    all_to_all x1, blocking collectives, local(): lax.all_to_all(k_in[0], 'seq', split_axis=1, concat_axis=0, tiled=True)  54.5 us
    all_to_all x1, blocking collectives, local(): lax.all_to_all(v_in[0], 'seq', split_axis=1, concat_axis=0, tiled=True)  51 us
    all_to_all x1, waiting for transfers between devices, local(): lax.all_to_all(q_in[0], 'seq', split_axis=1, concat_axis=0, tiled=True)  47.3 us
    all_to_all x1, waiting for transfers between devices, local(): lax.all_to_all(attn, 'seq', split_axis=0, concat_axis=1, tiled=True)  47.3 us
    reduce_sum x8, other arithmetic, one_block(): total = total * shrink + jnp.sum(expo, axis=-1)  37 us
    dynamic_slice x16, local copies, waits for them, and re-layouts, one_block(): lax.dynamic_slice_in_dim(value_piece, offset, block, 0)  25.8 us
  transfers between devices with their start and end apart: 4, of which 3 were waited for; matrix products, arithmetic and copies ran while one was open for 2% of the time, Pallas kernels for 0%

commit v1 on v0

--- a/solution.py
+++ b/solution.py
@@ -1,3 +1,4 @@
+import functools
 import math
 import jax
 import jax.numpy as jnp
@@ -8,11 +9,23 @@
 masked_score = -1e30
 
 
+def _finish_keys(u_in, link_axis):
+    item_now = jax.lax.psum(1, axis_name=link_axis)
+    built = jnp.split(u_in, item_now, axis=1)
+    t_next = jnp.stack(built, axis=0)
+    lower = jax.lax.all_to_all(t_next, axis_name=link_axis, split_axis=0, concat_axis=0)
+    then = jnp.concatenate(lower, axis=0)
+    return then
+
+
+axis_part_register = functools.partial(_finish_keys, link_axis="seq")
+
+
 def local(q_in, k_in, v_in, timesteps, gate_table):
     head_rows, key_rows, value_rows = (
         lax.all_to_all(q_in[0], "seq", split_axis=1, concat_axis=0, tiled=True),
         lax.all_to_all(k_in[0], "seq", split_axis=1, concat_axis=0, tiled=True),
-        lax.all_to_all(v_in[0], "seq", split_axis=1, concat_axis=0, tiled=True),
+        axis_part_register(v_in[0]),
     )
     length = head_rows.shape[0]
     columns = head_rows.shape[1]

time: 536 us -> 513 us (0.957)
  local copies, waits for them, and re-layouts: 84 us -> 61 us
    dynamic_slice x16 -> x8, local copies, waits for them, and re-layouts: 25.8 us -> 11.6 us  [one_block(): lax.dynamic_slice_in_dim(value_piece, offset, block, 0)]
    while x24 -> x72, local copies, waits for them, and re-layouts: 9.48 us -> 0.18 us
    unnamed x7 -> x6, local copies, waits for them, and re-layouts: 12.3 us -> 8.16 us
    dynamic_slice x8 -> x16, local copies, waits for them, and re-layouts: 11.9 us -> 14.7 us  [one_block(): lax.dynamic_slice_in_dim(key_piece, offset, block, 0)]
where the time goes in v1:
time: 513 us; the launch traced here: 511 us
  matrix products  171 us (33%)
  blocking collectives  105 us (20%)
  waiting for transfers between devices  99.6 us (19%)
  local copies, waits for them, and re-layouts  61 us (12%)
  other arithmetic  51.8 us (10%)
  between operations  13.5 us (3%)
  starting transfers between devices  8.25 us (2%)
    dot_general x8, matrix products, one_block(): jnp.einsum('hqk,khd->qhd', expo.astype(jnp.bfloat16), value_block, prefer...  95.1 us
    dot_general x8, matrix products, one_block(): jnp.einsum('qhd,khd->hqk', query_three, key_block, preferred_element_type...  75.2 us
    all_to_all x1, blocking collectives, _finish_keys(): jax.lax.all_to_all(t_next, axis_name=link_axis, split_axis=0, concat_axis=0)  54.3 us
    all_to_all x1, blocking collectives, local(): lax.all_to_all(k_in[0], 'seq', split_axis=1, concat_axis=0, tiled=True)  51 us
    all_to_all x1, waiting for transfers between devices, local(): lax.all_to_all(q_in[0], 'seq', split_axis=1, concat_axis=0, tiled=True)  47.3 us
    all_to_all x1, waiting for transfers between devices, local(): lax.all_to_all(attn, 'seq', split_axis=0, concat_axis=1, tiled=True)  47.3 us
    reduce_sum x8, other arithmetic, one_block(): total = total * shrink + jnp.sum(expo, axis=-1)  37.1 us
    dynamic_slice x16, local copies, waits for them, and re-layouts, one_block(): lax.dynamic_slice_in_dim(key_piece, offset, block, 0)  14.7 us
  transfers between devices with their start and end apart: 4, of which 3 were waited for; matrix products, arithmetic and copies ran while one was open for 2% of the time, Pallas kernels for 0%

profile of v1, /device:TPU:0, one launch (start us, length us, event | category | flops | bytes accessed | tf_op | source)
XLA Modules:
  0.0 511.4 jit_solution(11278586858821618686)
XLA Ops:
  8.6 54.3 %all_to_all.50 = bf16[4,256,1024]{2,1,0:T(8,128)(2,1)S(1)} all-to-all(bf16[4,256,1024]{2,1,0:T(8,128)(2,1)S(1)} %pad_maximum_fusion), channel_id=1, replica_groups=mesh['parts'=2,'span'=4,'seq'=4] {'seq'}, dimensions={0} | all-to-all | bytes 4194304 | tf_op jit(solution)/shard_map/all_to_all | solution.py:16
  69.6 51.0 %all_to_all.51 = bf16[256,4,1024]{0,2,1:T(8,128)(2,1)S(1)} all-to-all(bf16[256,4,1024]{0,2,1:T(8,128)(2,1)} %bitcast.88), channel_id=1, replica_groups=mesh['parts'=2,'span'=4,'seq'=4] {'seq'}, dimensions={1} | all-to-all | bytes 4194304 | tf_op jit(solution)/shard_map/all_to_all | solution.py:27
  130.7 47.3 %all-to-all-done = bf16[256,4,1024]{0,2,1:T(8,128)(2,1)S(1)} async-done(((bf16[256,4,1024]{0,2,1:T(8,128)(2,1)}), bf16[256,4,1024]{0,2,1:T(8,128)(2,1)S(1)}, u32[]{:S(2)}, u32[]{:S(2)}) %all-to-all-start) | async-done | bytes 2097184 | tf_op jit(solution)/shard_map/all_to_all | solution.py:26
  178.0 5.0 all-gather.3.cloned.1.call-done
  183.0 251.4 %conditional.1 = (f32[8,1024]{1,0:T(8,128)}, f32[1024,8,128]{0,2,1:T(8,128)}) conditional(s32[]{:T(128)} %convert_element_type.44, () %tuple.27, (bf16[4,256,1024]{1,2,0:T(8,128)(2,1)S(1)}, s32[]{:T(128)}, bf16[4096,1024]{1,0:T(8,128)(2,1)}, bf16[4096,1024]{0,1:T(8,128)(2,1)}) %tuple.65), branch_computations={%region_0.0_spmd, %region_1.6_spmd} | conditional | flops 2205205504 | bytes 132647312 | solution.py:79
  189.3 245.1 %while.17 = (s32[]{:T(128)}, f32[8,1024]{1,0:T(8,128)S(1)}, f32[8,1024]{1,0:T(8,128)}, f32[1024,8,128]{0,2,1:T(8,128)}, s32[]{:T(128)}, /*index=5*/bf16[4096,102...) while((s32[]{:T(128)}, f32[8,1024]{1,0:T(8,128)S(1)}, ...), condition=%wide.region_5.5_spmd.clone, body=%wide.region_2.4_spmd.clone.sunk | while | flops 2205205504 | bytes 120064280 | solution.py:74
  191.1 9.4 %bitcast_reduce_fusion.2 = (f32[8,1024]{1,0:T(8,128)S(1)}, f32[8,512,1024]{2,1,0:T(8,128)}) fusion(pred[512]{0:T(512)(128)(4,1)S(1)} %add_compare_fusion.2, bf16[512,8,128]{0,2,1:T(8,128)(2,1)S(1)} %bitcast.80, bf16[1024,8,128]{2,0,1:T(8,128)(2,1)} %get-tuple-element.336), kind=kOutput, calls=%fused_computation.1.clone.1 | convolution fusion | flops 1086316544 | bytes 19956224 | tf_op jit(solution)/shard_map/cond/branch_1_fun/while/body/eval_jaxpr/qhd,khd->hqk/dot_general | solution.py:55
  202.0 10.8 %bitcast_add_fusion.2 = f32[1024,8,128]{0,2,1:T(8,128)} fusion(f32[1024,8,128]{0,2,1:T(8,128)} %get-tuple-element.321, bf16[512,8,128]{0,2,1:T(8,128)(2,1)S(1)} %bitcast.81, f32[8,512,1024]{2,1,0:T(8,128)} %get-tuple-element.304, f32[8,1024]{1,0:T(8,128)S(1)} %get-tuple-element.331, pred[512]{0:T(512)(128)(4,1)S(1)} %add_compare_fusion.2, ...), kind=kOutput, calls=%fused_computation.10.clone.1 | convolution fusion | flops 1097859072 | bytes 26280448 | tf_op jit(solution)/shard_map/cond/branch_1_fun/while/body/eval_jaxpr/hqk,khd->qhd/dot_general | solution.py:64
  212.9 4.6 fusion.37
  220.1 9.4 %bitcast_reduce_fusion.2 = (f32[8,1024]{1,0:T(8,128)S(1)}, f32[8,512,1024]{2,1,0:T(8,128)}) fusion(pred[512]{0:T(512)(128)(4,1)S(1)} %add_compare_fusion.2, bf16[512,8,128]{0,2,1:T(8,128)(2,1)S(1)} %bitcast.80, bf16[1024,8,128]{2,0,1:T(8,128)(2,1)} %get-tuple-element.336), kind=kOutput, calls=%fused_computation.1.clone.1 | convolution fusion | flops 1086316544 | bytes 19956224 | tf_op jit(solution)/shard_map/cond/branch_1_fun/while/body/eval_jaxpr/qhd,khd->hqk/dot_general | solution.py:55
  231.0 12.0 %bitcast_add_fusion.2 = f32[1024,8,128]{0,2,1:T(8,128)} fusion(f32[1024,8,128]{0,2,1:T(8,128)} %get-tuple-element.321, bf16[512,8,128]{0,2,1:T(8,128)(2,1)S(1)} %bitcast.81, f32[8,512,1024]{2,1,0:T(8,128)} %get-tuple-element.304, f32[8,1024]{1,0:T(8,128)S(1)} %get-tuple-element.331, pred[512]{0:T(512)(128)(4,1)S(1)} %add_compare_fusion.2, ...), kind=kOutput, calls=%fused_computation.10.clone.1 | convolution fusion | flops 1097859072 | bytes 26280448 | tf_op jit(solution)/shard_map/cond/branch_1_fun/while/body/eval_jaxpr/hqk,khd->qhd/dot_general | solution.py:64
  243.0 4.6 fusion.37
  251.0 9.4 %bitcast_reduce_fusion.2 = (f32[8,1024]{1,0:T(8,128)S(1)}, f32[8,512,1024]{2,1,0:T(8,128)}) fusion(pred[512]{0:T(512)(128)(4,1)S(1)} %add_compare_fusion.2, bf16[512,8,128]{0,2,1:T(8,128)(2,1)S(1)} %bitcast.80, bf16[1024,8,128]{2,0,1:T(8,128)(2,1)} %get-tuple-element.336), kind=kOutput, calls=%fused_computation.1.clone.1 | convolution fusion | flops 1086316544 | bytes 19956224 | tf_op jit(solution)/shard_map/cond/branch_1_fun/while/body/eval_jaxpr/qhd,khd->hqk/dot_general | solution.py:55
  261.9 12.0 %bitcast_add_fusion.2 = f32[1024,8,128]{0,2,1:T(8,128)} fusion(f32[1024,8,128]{0,2,1:T(8,128)} %get-tuple-element.321, bf16[512,8,128]{0,2,1:T(8,128)(2,1)S(1)} %bitcast.81, f32[8,512,1024]{2,1,0:T(8,128)} %get-tuple-element.304, f32[8,1024]{1,0:T(8,128)S(1)} %get-tuple-element.331, pred[512]{0:T(512)(128)(4,1)S(1)} %add_compare_fusion.2, ...), kind=kOutput, calls=%fused_computation.10.clone.1 | convolution fusion | flops 1097859072 | bytes 26280448 | tf_op jit(solution)/shard_map/cond/branch_1_fun/while/body/eval_jaxpr/hqk,khd->qhd/dot_general | solution.py:64
  273.9 4.6 fusion.37
  281.8 9.4 %bitcast_reduce_fusion.2 = (f32[8,1024]{1,0:T(8,128)S(1)}, f32[8,512,1024]{2,1,0:T(8,128)}) fusion(pred[512]{0:T(512)(128)(4,1)S(1)} %add_compare_fusion.2, bf16[512,8,128]{0,2,1:T(8,128)(2,1)S(1)} %bitcast.80, bf16[1024,8,128]{2,0,1:T(8,128)(2,1)} %get-tuple-element.336), kind=kOutput, calls=%fused_computation.1.clone.1 | convolution fusion | flops 1086316544 | bytes 19956224 | tf_op jit(solution)/shard_map/cond/branch_1_fun/while/body/eval_jaxpr/qhd,khd->hqk/dot_general | solution.py:55
  292.7 12.0 %bitcast_add_fusion.2 = f32[1024,8,128]{0,2,1:T(8,128)} fusion(f32[1024,8,128]{0,2,1:T(8,128)} %get-tuple-element.321, bf16[512,8,128]{0,2,1:T(8,128)(2,1)S(1)} %bitcast.81, f32[8,512,1024]{2,1,0:T(8,128)} %get-tuple-element.304, f32[8,1024]{1,0:T(8,128)S(1)} %get-tuple-element.331, pred[512]{0:T(512)(128)(4,1)S(1)} %add_compare_fusion.2, ...), kind=kOutput, calls=%fused_computation.10.clone.1 | convolution fusion | flops 1097859072 | bytes 26280448 | tf_op jit(solution)/shard_map/cond/branch_1_fun/while/body/eval_jaxpr/hqk,khd->qhd/dot_general | solution.py:64
  304.8 4.6 fusion.37
  312.7 9.4 %bitcast_reduce_fusion.2 = (f32[8,1024]{1,0:T(8,128)S(1)}, f32[8,512,1024]{2,1,0:T(8,128)}) fusion(pred[512]{0:T(512)(128)(4,1)S(1)} %add_compare_fusion.2, bf16[512,8,128]{0,2,1:T(8,128)(2,1)S(1)} %bitcast.80, bf16[1024,8,128]{2,0,1:T(8,128)(2,1)} %get-tuple-element.336), kind=kOutput, calls=%fused_computation.1.clone.1 | convolution fusion | flops 1086316544 | bytes 19956224 | tf_op jit(solution)/shard_map/cond/branch_1_fun/while/body/eval_jaxpr/qhd,khd->hqk/dot_general | solution.py:55
  323.6 12.0 %bitcast_add_fusion.2 = f32[1024,8,128]{0,2,1:T(8,128)} fusion(f32[1024,8,128]{0,2,1:T(8,128)} %get-tuple-element.321, bf16[512,8,128]{0,2,1:T(8,128)(2,1)S(1)} %bitcast.81, f32[8,512,1024]{2,1,0:T(8,128)} %get-tuple-element.304, f32[8,1024]{1,0:T(8,128)S(1)} %get-tuple-element.331, pred[512]{0:T(512)(128)(4,1)S(1)} %add_compare_fusion.2, ...), kind=kOutput, calls=%fused_computation.10.clone.1 | convolution fusion | flops 1097859072 | bytes 26280448 | tf_op jit(solution)/shard_map/cond/branch_1_fun/while/body/eval_jaxpr/hqk,khd->qhd/dot_general | solution.py:64
  335.7 4.6 fusion.37
  343.6 9.4 %bitcast_reduce_fusion.2 = (f32[8,1024]{1,0:T(8,128)S(1)}, f32[8,512,1024]{2,1,0:T(8,128)}) fusion(pred[512]{0:T(512)(128)(4,1)S(1)} %add_compare_fusion.2, bf16[512,8,128]{0,2,1:T(8,128)(2,1)S(1)} %bitcast.80, bf16[1024,8,128]{2,0,1:T(8,128)(2,1)} %get-tuple-element.336), kind=kOutput, calls=%fused_computation.1.clone.1 | convolution fusion | flops 1086316544 | bytes 19956224 | tf_op jit(solution)/shard_map/cond/branch_1_fun/while/body/eval_jaxpr/qhd,khd->hqk/dot_general | solution.py:55
  354.5 12.0 %bitcast_add_fusion.2 = f32[1024,8,128]{0,2,1:T(8,128)} fusion(f32[1024,8,128]{0,2,1:T(8,128)} %get-tuple-element.321, bf16[512,8,128]{0,2,1:T(8,128)(2,1)S(1)} %bitcast.81, f32[8,512,1024]{2,1,0:T(8,128)} %get-tuple-element.304, f32[8,1024]{1,0:T(8,128)S(1)} %get-tuple-element.331, pred[512]{0:T(512)(128)(4,1)S(1)} %add_compare_fusion.2, ...), kind=kOutput, calls=%fused_computation.10.clone.1 | convolution fusion | flops 1097859072 | bytes 26280448 | tf_op jit(solution)/shard_map/cond/branch_1_fun/while/body/eval_jaxpr/hqk,khd->qhd/dot_general | solution.py:64
  366.6 4.6 fusion.37
  374.5 9.4 %bitcast_reduce_fusion.2 = (f32[8,1024]{1,0:T(8,128)S(1)}, f32[8,512,1024]{2,1,0:T(8,128)}) fusion(pred[512]{0:T(512)(128)(4,1)S(1)} %add_compare_fusion.2, bf16[512,8,128]{0,2,1:T(8,128)(2,1)S(1)} %bitcast.80, bf16[1024,8,128]{2,0,1:T(8,128)(2,1)} %get-tuple-element.336), kind=kOutput, calls=%fused_computation.1.clone.1 | convolution fusion | flops 1086316544 | bytes 19956224 | tf_op jit(solution)/shard_map/cond/branch_1_fun/while/body/eval_jaxpr/qhd,khd->hqk/dot_general | solution.py:55
  385.4 12.0 %bitcast_add_fusion.2 = f32[1024,8,128]{0,2,1:T(8,128)} fusion(f32[1024,8,128]{0,2,1:T(8,128)} %get-tuple-element.321, bf16[512,8,128]{0,2,1:T(8,128)(2,1)S(1)} %bitcast.81, f32[8,512,1024]{2,1,0:T(8,128)} %get-tuple-element.304, f32[8,1024]{1,0:T(8,128)S(1)} %get-tuple-element.331, pred[512]{0:T(512)(128)(4,1)S(1)} %add_compare_fusion.2, ...), kind=kOutput, calls=%fused_computation.10.clone.1 | convolution fusion | flops 1097859072 | bytes 26280448 | tf_op jit(solution)/shard_map/cond/branch_1_fun/while/body/eval_jaxpr/hqk,khd->qhd/dot_general | solution.py:64
  397.5 4.6 fusion.37
  405.4 9.4 %bitcast_reduce_fusion.2 = (f32[8,1024]{1,0:T(8,128)S(1)}, f32[8,512,1024]{2,1,0:T(8,128)}) fusion(pred[512]{0:T(512)(128)(4,1)S(1)} %add_compare_fusion.2, bf16[512,8,128]{0,2,1:T(8,128)(2,1)S(1)} %bitcast.80, bf16[1024,8,128]{2,0,1:T(8,128)(2,1)} %get-tuple-element.336), kind=kOutput, calls=%fused_computation.1.clone.1 | convolution fusion | flops 1086316544 | bytes 19956224 | tf_op jit(solution)/shard_map/cond/branch_1_fun/while/body/eval_jaxpr/qhd,khd->hqk/dot_general | solution.py:55
  416.3 12.0 %bitcast_add_fusion.2 = f32[1024,8,128]{0,2,1:T(8,128)} fusion(f32[1024,8,128]{0,2,1:T(8,128)} %get-tuple-element.321, bf16[512,8,128]{0,2,1:T(8,128)(2,1)S(1)} %bitcast.81, f32[8,512,1024]{2,1,0:T(8,128)} %get-tuple-element.304, f32[8,1024]{1,0:T(8,128)S(1)} %get-tuple-element.331, pred[512]{0:T(512)(128)(4,1)S(1)} %add_compare_fusion.2, ...), kind=kOutput, calls=%fused_computation.10.clone.1 | convolution fusion | flops 1097859072 | bytes 26280448 | tf_op jit(solution)/shard_map/cond/branch_1_fun/while/body/eval_jaxpr/hqk,khd->qhd/dot_general | solution.py:64
  428.4 4.6 fusion.37
  444.3 4.6 all-to-all-start.3
  450.4 47.3 %all-to-all-done.3 = bf16[4,256,1024]{2,1,0:T(8,128)(2,1)} async-done(((bf16[4,256,1024]{2,1,0:T(8,128)(2,1)}), bf16[4,256,1024]{2,1,0:T(8,128)(2,1)}, u32[]{:S(2)}, u32[]{:S(2)}) %all-to-all-start.3) | async-done | bytes 2097184 | tf_op jit(solution)/shard_map/all_to_all | solution.py:81
  (159 shorter events, 80.3 us)
Async XLA Ops:
  6.5 443.0 %copy-start = (f32[32,4096]{1,0:T(8,128)S(1)}, f32[32,4096]{1,0:T(8,128)}, u32[]{:S(2)}) copy-start(f32[32,4096]{1,0:T(8,128)} %param.13) | copy-start | bytes 1572868
  6.5 171.5 %all-gather.5.cloned.1.call-start = ((), (), s32[]{:S(2)}) async-start(), calls=%async_computation.5 | async-start | bytes 10485760 | tf_op jit(solution)/shard_map/all_gather | solution.py:43
  65.5 117.5 %all-gather.3.cloned.1.call-start = ((), (), s32[]{:S(2)}) async-start(), calls=%async_computation.4 | async-start | bytes 10485760 | tf_op jit(solution)/shard_map/all_gather | solution.py:42
  127.1 50.9 %all-to-all-start = ((bf16[256,4,1024]{0,2,1:T(8,128)(2,1)}), bf16[256,4,1024]{0,2,1:T(8,128)(2,1)S(1)}, u32[]{:S(2)}, u32[]{:S(2)}) async-start(bf16[256,4,1024]{0,2,1:T(8,128)(2,1)} %bitcast.85), calls=%async_computation | async-start | bytes 4194304 | tf_op jit(solution)/shard_map/all_to_all | solution.py:26
  200.5 12.3 %slice-start = ((s8[16777216]{0:T(1024)(128)(4,1)}), s8[4194304]{0:T(1024)(128)(4,1)S(1)}, s32[]{:S(2)}) async-start(s8[16777216]{0:T(1024)(128)(4,1)} %bitcast.78), calls=%async_computation.6 | async-start | bytes 8388608 | tf_op jit(solution)/shard_map/cond/branch_1_fun/while
  229.5 13.5 %slice-start = ((s8[16777216]{0:T(1024)(128)(4,1)}), s8[4194304]{0:T(1024)(128)(4,1)S(1)}, s32[]{:S(2)}) async-start(s8[16777216]{0:T(1024)(128)(4,1)} %bitcast.78), calls=%async_computation.6 | async-start | bytes 8388608 | tf_op jit(solution)/shard_map/cond/branch_1_fun/while
  230.9 12.1 %slice-start.1 = ((s8[16777216]{0:T(1024)(128)(4,1)}), s8[4194304]{0:T(1024)(128)(4,1)S(1)}, s32[]{:S(2)}) async-start(s8[16777216]{0:T(1024)(128)(4,1)} %bitcast.78), calls=%async_computation.7 | async-start | bytes 8388608 | tf_op jit(solution)/shard_map/cond/branch_1_fun/while
  231.0 12.1 %slice-start.2 = ((s8[16777216]{0:T(1024)(128)(4,1)}), s8[4194304]{0:T(1024)(128)(4,1)S(1)}, s32[]{:S(2)}) async-start(s8[16777216]{0:T(1024)(128)(4,1)} %bitcast.78), calls=%async_computation.8 | async-start | bytes 8388608 | tf_op jit(solution)/shard_map/cond/branch_1_fun/while
  231.0 12.1 %slice-start.3 = ((s8[16777216]{0:T(1024)(128)(4,1)}), s8[4194304]{0:T(1024)(128)(4,1)S(1)}, s32[]{:S(2)}) async-start(s8[16777216]{0:T(1024)(128)(4,1)} %bitcast.78), calls=%async_computation.9 | async-start | bytes 8388608 | tf_op jit(solution)/shard_map/cond/branch_1_fun/while
  260.4 13.5 %slice-start = ((s8[16777216]{0:T(1024)(128)(4,1)}), s8[4194304]{0:T(1024)(128)(4,1)S(1)}, s32[]{:S(2)}) async-start(s8[16777216]{0:T(1024)(128)(4,1)} %bitcast.78), calls=%async_computation.6 | async-start | bytes 8388608 | tf_op jit(solution)/shard_map/cond/branch_1_fun/while
  261.8 12.1 %slice-start.1 = ((s8[16777216]{0:T(1024)(128)(4,1)}), s8[4194304]{0:T(1024)(128)(4,1)S(1)}, s32[]{:S(2)}) async-start(s8[16777216]{0:T(1024)(128)(4,1)} %bitcast.78), calls=%async_computation.7 | async-start | bytes 8388608 | tf_op jit(solution)/shard_map/cond/branch_1_fun/while
  261.8 12.1 %slice-start.2 = ((s8[16777216]{0:T(1024)(128)(4,1)}), s8[4194304]{0:T(1024)(128)(4,1)S(1)}, s32[]{:S(2)}) async-start(s8[16777216]{0:T(1024)(128)(4,1)} %bitcast.78), calls=%async_computation.8 | async-start | bytes 8388608 | tf_op jit(solution)/shard_map/cond/branch_1_fun/while
  261.9 12.1 %slice-start.3 = ((s8[16777216]{0:T(1024)(128)(4,1)}), s8[4194304]{0:T(1024)(128)(4,1)S(1)}, s32[]{:S(2)}) async-start(s8[16777216]{0:T(1024)(128)(4,1)} %bitcast.78), calls=%async_computation.9 | async-start | bytes 8388608 | tf_op jit(solution)/shard_map/cond/branch_1_fun/while
  291.3 13.5 %slice-start = ((s8[16777216]{0:T(1024)(128)(4,1)}), s8[4194304]{0:T(1024)(128)(4,1)S(1)}, s32[]{:S(2)}) async-start(s8[16777216]{0:T(1024)(128)(4,1)} %bitcast.78), calls=%async_computation.6 | async-start | bytes 8388608 | tf_op jit(solution)/shard_map/cond/branch_1_fun/while
  292.7 12.1 %slice-start.1 = ((s8[16777216]{0:T(1024)(128)(4,1)}), s8[4194304]{0:T(1024)(128)(4,1)S(1)}, s32[]{:S(2)}) async-start(s8[16777216]{0:T(1024)(128)(4,1)} %bitcast.78), calls=%async_computation.7 | async-start | bytes 8388608 | tf_op jit(solution)/shard_map/cond/branch_1_fun/while
  292.7 12.1 %slice-start.2 = ((s8[16777216]{0:T(1024)(128)(4,1)}), s8[4194304]{0:T(1024)(128)(4,1)S(1)}, s32[]{:S(2)}) async-start(s8[16777216]{0:T(1024)(128)(4,1)} %bitcast.78), calls=%async_computation.8 | async-start | bytes 8388608 | tf_op jit(solution)/shard_map/cond/branch_1_fun/while
  292.7 12.1 %slice-start.3 = ((s8[16777216]{0:T(1024)(128)(4,1)}), s8[4194304]{0:T(1024)(128)(4,1)S(1)}, s32[]{:S(2)}) async-start(s8[16777216]{0:T(1024)(128)(4,1)} %bitcast.78), calls=%async_computation.9 | async-start | bytes 8388608 | tf_op jit(solution)/shard_map/cond/branch_1_fun/while
  322.1 13.5 %slice-start = ((s8[16777216]{0:T(1024)(128)(4,1)}), s8[4194304]{0:T(1024)(128)(4,1)S(1)}, s32[]{:S(2)}) async-start(s8[16777216]{0:T(1024)(128)(4,1)} %bitcast.78), calls=%async_computation.6 | async-start | bytes 8388608 | tf_op jit(solution)/shard_map/cond/branch_1_fun/while
  323.6 12.1 %slice-start.1 = ((s8[16777216]{0:T(1024)(128)(4,1)}), s8[4194304]{0:T(1024)(128)(4,1)S(1)}, s32[]{:S(2)}) async-start(s8[16777216]{0:T(1024)(128)(4,1)} %bitcast.78), calls=%async_computation.7 | async-start | bytes 8388608 | tf_op jit(solution)/shard_map/cond/branch_1_fun/while
  323.6 12.1 %slice-start.2 = ((s8[16777216]{0:T(1024)(128)(4,1)}), s8[4194304]{0:T(1024)(128)(4,1)S(1)}, s32[]{:S(2)}) async-start(s8[16777216]{0:T(1024)(128)(4,1)} %bitcast.78), calls=%async_computation.8 | async-start | bytes 8388608 | tf_op jit(solution)/shard_map/cond/branch_1_fun/while
  323.6 12.1 %slice-start.3 = ((s8[16777216]{0:T(1024)(128)(4,1)}), s8[4194304]{0:T(1024)(128)(4,1)S(1)}, s32[]{:S(2)}) async-start(s8[16777216]{0:T(1024)(128)(4,1)} %bitcast.78), calls=%async_computation.9 | async-start | bytes 8388608 | tf_op jit(solution)/shard_map/cond/branch_1_fun/while
  353.0 13.5 %slice-start = ((s8[16777216]{0:T(1024)(128)(4,1)}), s8[4194304]{0:T(1024)(128)(4,1)S(1)}, s32[]{:S(2)}) async-start(s8[16777216]{0:T(1024)(128)(4,1)} %bitcast.78), calls=%async_computation.6 | async-start | bytes 8388608 | tf_op jit(solution)/shard_map/cond/branch_1_fun/while
  354.5 12.1 %slice-start.1 = ((s8[16777216]{0:T(1024)(128)(4,1)}), s8[4194304]{0:T(1024)(128)(4,1)S(1)}, s32[]{:S(2)}) async-start(s8[16777216]{0:T(1024)(128)(4,1)} %bitcast.78), calls=%async_computation.7 | async-start | bytes 8388608 | tf_op jit(solution)/shard_map/cond/branch_1_fun/while
  354.5 12.1 %slice-start.2 = ((s8[16777216]{0:T(1024)(128)(4,1)}), s8[4194304]{0:T(1024)(128)(4,1)S(1)}, s32[]{:S(2)}) async-start(s8[16777216]{0:T(1024)(128)(4,1)} %bitcast.78), calls=%async_computation.8 | async-start | bytes 8388608 | tf_op jit(solution)/shard_map/cond/branch_1_fun/while
  383.9 13.5 %slice-start = ((s8[16777216]{0:T(1024)(128)(4,1)}), s8[4194304]{0:T(1024)(128)(4,1)S(1)}, s32[]{:S(2)}) async-start(s8[16777216]{0:T(1024)(128)(4,1)} %bitcast.78), calls=%async_computation.6 | async-start | bytes 8388608 | tf_op jit(solution)/shard_map/cond/branch_1_fun/while
  385.4 12.1 %slice-start.1 = ((s8[16777216]{0:T(1024)(128)(4,1)}), s8[4194304]{0:T(1024)(128)(4,1)S(1)}, s32[]{:S(2)}) async-start(s8[16777216]{0:T(1024)(128)(4,1)} %bitcast.78), calls=%async_computation.7 | async-start | bytes 8388608 | tf_op jit(solution)/shard_map/cond/branch_1_fun/while
  385.4 12.1 %slice-start.2 = ((s8[16777216]{0:T(1024)(128)(4,1)}), s8[4194304]{0:T(1024)(128)(4,1)S(1)}, s32[]{:S(2)}) async-start(s8[16777216]{0:T(1024)(128)(4,1)} %bitcast.78), calls=%async_computation.8 | async-start | bytes 8388608 | tf_op jit(solution)/shard_map/cond/branch_1_fun/while
  385.4 12.1 %slice-start.3 = ((s8[16777216]{0:T(1024)(128)(4,1)}), s8[4194304]{0:T(1024)(128)(4,1)S(1)}, s32[]{:S(2)}) async-start(s8[16777216]{0:T(1024)(128)(4,1)} %bitcast.78), calls=%async_computation.9 | async-start | bytes 8388608 | tf_op jit(solution)/shard_map/cond/branch_1_fun/while
  414.8 13.5 %slice-start = ((s8[16777216]{0:T(1024)(128)(4,1)}), s8[4194304]{0:T(1024)(128)(4,1)S(1)}, s32[]{:S(2)}) async-start(s8[16777216]{0:T(1024)(128)(4,1)} %bitcast.78), calls=%async_computation.6 | async-start | bytes 8388608 | tf_op jit(solution)/shard_map/cond/branch_1_fun/while
  416.3 12.1 %slice-start.1 = ((s8[16777216]{0:T(1024)(128)(4,1)}), s8[4194304]{0:T(1024)(128)(4,1)S(1)}, s32[]{:S(2)}) async-start(s8[16777216]{0:T(1024)(128)(4,1)} %bitcast.78), calls=%async_computation.7 | async-start | bytes 8388608 | tf_op jit(solution)/shard_map/cond/branch_1_fun/while
  416.3 12.1 %slice-start.2 = ((s8[16777216]{0:T(1024)(128)(4,1)}), s8[4194304]{0:T(1024)(128)(4,1)S(1)}, s32[]{:S(2)}) async-start(s8[16777216]{0:T(1024)(128)(4,1)} %bitcast.78), calls=%async_computation.8 | async-start | bytes 8388608 | tf_op jit(solution)/shard_map/cond/branch_1_fun/while
  444.3 53.4 %all-to-all-start.3 = ((bf16[4,256,1024]{2,1,0:T(8,128)(2,1)}), bf16[4,256,1024]{2,1,0:T(8,128)(2,1)}, u32[]{:S(2)}, u32[]{:S(2)}) async-start(bf16[4,256,1024]{2,1,0:T(8,128)(2,1)} %copy.41), calls=%async_computation.3 | async-start | bytes 4194304 | tf_op jit(solution)/shard_map/all_to_all | solution.py:81
  (6 other events, 65.7 us)
Sparse Core Ops, SparseCore 0:
  65.6 57.4 all-gather.4
  124.7 58.2 all-gather.2
